TPU v7x, 32 devices: a whole 2x2x4 slice. The times are simulated.
32 devices in a mesh: gx: 4 (over x, core), gy: 8 (over z, y).
Axes of the slice: x: 2, y: 2, z: 4, core: 2. Of those that a mesh axis runs over, the one named last changes fastest.
Arguments:
- direct: float32 [4, 4, 8, 1024], P(None, 'gx', 'gy'), may hold values from 0 to 1
- omega: float32 [3, 4, 8, 1024], P(None, 'gx', 'gy'), may hold values from 0.1 to 0.9
- band_sun: float32 [3, 4], replicated, may hold values from 0.5 to 2
- air_temp: float32 [4], replicated, may hold values from 15 to 35
- vcmax: float32 [4, 8, 1024], P('gx', 'gy'), may hold values from 0.4 to 1.6
- self_view: bfloat16 [4, 8, 1024, 1024], P('gx', 'gy'), may hold values from 1e-07 to 0.0401
- near_view: bfloat16 [4, 8, 8, 1024, 1024], P('gx', 'gy'), may hold values from 1e-07 to 0.0401
- near_ids: int32 [4, 8, 8], P('gx', 'gy'), may hold values from 0 to 31, as said below
- organ_of_patch: int32 [4, 8, 1024], P('gx', 'gy'), may hold values from 0 to 1279
- organ_plant: int32 [1280], replicated, may hold values from 0 to 159
Outputs:
- assimilation: float32 [4, 8, 1024], P('gx', 'gy')
- organ_carbon: float32 [1280], P(('gx', 'gy'))
- plant_carbon: float32 [160], P(('gx', 'gy'))
Inputs may be any that keep to these rules, and one draw needn't show every extreme that they name: `near_ids`: the 8 ids of a block are distinct, differ from the block itself, and lie within two block rows and two block columns of it.
All inputs are finite; a program needn't handle non-finite values.
Results may differ from a plain program's by a relative error of at most 0.0003.
Values may be sent and summed in bfloat16 or wider, within the bound.
A program may use at most 64 MiB of HBM per device.

v0:
```python
import jax
import jax.numpy as jnp
from jax import lax
from jax.sharding import PartitionSpec as P

SWEEPS = 2
ORG_PER = 8


def assimilate(absorbed, vcmax, air_temp):
    shape = (air_temp.shape[0],) + (1,) * (absorbed.ndim - 2)
    heat = absorbed[1] + absorbed[2]
    leaf_temp = air_temp.reshape(shape) + 6.0 * heat
    capacity = vcmax[None] * jnp.exp(0.07 * (leaf_temp - 25.0))
    jmax = 1.7 * capacity
    light = 1.5 * absorbed[0]
    total = light + jmax
    elec = (total - jnp.sqrt(total * total - 2.8 * light * jmax)) / 1.4
    carbox = capacity * (0.7 - 0.05) / (0.7 + 0.5)
    electron = elec * (0.7 - 0.05) / (0.7 + 0.1)
    net_rate = jnp.minimum(carbox, electron) - 0.015 * capacity
    return 0.25 * jnp.sum(net_rate, axis=0)


def fetch_neighbours(sent, ids, rows, cols):
    whole = lax.all_gather(sent, ("gx", "gy"), axis=1, tiled=True)
    block_row = ids // cols
    position = (block_row // rows * cols + ids % cols) * rows + block_row % rows
    return jnp.take(whole, position, axis=1)


def shards(
    direct,
    omega,
    band_sun,
    air_temp,
    vcmax,
    self_view,
    near_view,
    near_ids,
    organ_of_patch,
    organ_plant,
):
    rows = self_view.shape[0]
    width = self_view.shape[-1]
    cols = lax.axis_size("gy")
    bands = omega.shape[0]
    suns = direct.shape[0]
    own_views = self_view.reshape(rows, width, width)
    far_views = near_view.reshape(rows, near_ids.shape[-1], width, width)
    ids = near_ids.reshape(rows, -1)
    source = (band_sun[:, :, None, None, None] * direct[None]).reshape(bands * suns, rows, width)
    albedo = jnp.broadcast_to(omega, (bands, suns, rows, width)).reshape(bands * suns, rows, width)
    current = source
    scattered = source
    for sweep in range(SWEEPS):
        sent = current.astype(jnp.bfloat16)
        neighbours = fetch_neighbours(sent, ids, rows, cols)
        scattered = jnp.einsum("rpq,krq->krp", own_views, sent, preferred_element_type=jnp.float32)
        scattered = scattered + jnp.einsum(
            "rnpq,krnq->krp", far_views, neighbours, preferred_element_type=jnp.float32
        )
        current = source + albedo * scattered
    absorbed = ((1.0 - albedo) * (source + scattered)).reshape(bands, suns, rows, width)
    assimilation = assimilate(absorbed, vcmax.reshape(rows, width), air_temp)
    organs = organ_plant.shape[0]
    plants = organs // ORG_PER
    partial_value = jax.ops.segment_sum(
        assimilation.reshape(-1), organ_of_patch.reshape(-1), num_segments=organs
    )
    organ_share = lax.psum_scatter(partial_value, ("gx", "gy"), scatter_dimension=0, tiled=True)
    share_len = organ_share.shape[0]
    start = lax.axis_index(("gx", "gy")) * share_len
    owners = lax.dynamic_slice_in_dim(organ_plant, start, share_len, 0)
    plant_part = jax.ops.segment_sum(organ_share, owners, num_segments=plants)
    plant_share = lax.psum_scatter(plant_part, ("gx", "gy"), scatter_dimension=0, tiled=True)
    organ_carbon = 0.25 * organ_share
    plant_carbon = plant_share / 32.0
    return (assimilation.reshape(rows, 1, width), organ_carbon, plant_carbon)


def solution(mesh):
    return jax.shard_map(
        shards,
        mesh=mesh,
        in_specs=(
            P(None, "gx", "gy", None),
            P(None, "gx", "gy", None),
            P(),
            P(),
            P("gx", "gy", None),
            P("gx", "gy", None, None),
            P("gx", "gy", None, None, None),
            P("gx", "gy", None),
            P("gx", "gy", None),
            P(),
        ),
        out_specs=(P("gx", "gy", None), P(("gx", "gy")), P(("gx", "gy"))),
        check_vma=False,
    )
```

profile of v0, /device:TPU:0, one launch (start us, length us, event | category | flops | bytes accessed | tf_op | source)
XLA Modules:
  0.0 264.1 jit_solution(13954832389236116051)
XLA Ops:
  0.6 0.0 copy-start
  0.6 0.0 copy-start.3
  0.7 0.9 copy.20
  1.6 0.8 mul.195
  2.3 0.1 multiply_convert_fusion
  2.4 76.1 %all_gather.6 = bf16[12,32,1024]{2,0,1:T(8,128)(2,1)S(1)} all-gather(bf16[12,1,1024]{2,0,1:T(8,128)(2,1)S(1)} %multiply_convert_fusion), channel_id=1, replica_groups=mesh['gx'=4,'gy'=8] {'gx','gy'}, dimensions={1}, use_global_device_ids=true | all-gather | bytes 811008 | tf_op jit(solution)/shard_map/all_gather | solution.py:26
  78.5 0.7 and_bitcast_fusion
  79.2 0.6 gather_fusion
  79.7 10.2 %fusion.20 = f32[12,1024]{1,0:T(8,128)S(1)} fusion(bf16[1,1,8,1024,1024]{4,3,2,1,0:T(8,128)(2,1)} %param.18, bf16[8,12,1024]{2,1,0:T(8,128)(2,1)S(1)} %gather_fusion, pred[8]{0:T(512)(128)(4,1)S(1)} %get-tuple-element.6), kind=kOutput, calls=%fused_computation.16 | convolution fusion | flops 201424896 | bytes 17022984 | tf_op jit(solution)/shard_map/rnpq,krnq->krp/dot_general | solution.py:60
  89.9 0.0 copy-start.4
  89.9 0.0 copy-start.6
  90.0 0.0 copy-done.3
  90.1 0.0 copy-done
  90.1 0.0 copy-start.1
  90.1 0.6 fusion.32
  90.7 71.0 %all-gather = bf16[12,32768]{1,0:T(8,128)(2,1)S(1)} all-gather(bf16[12,1024]{1,0:T(8,128)(2,1)S(1)} %fusion.32), channel_id=2, replica_groups=mesh['gx'=4,'gy'=8] {'gx','gy'}, dimensions={1}, use_global_device_ids=true | all-gather | bytes 811008 | tf_op jit(solution)/shard_map/all_gather | solution.py:26
  161.7 0.6 copy.17
  162.3 0.0 copy-done.1
  162.3 0.1 slice.25
  162.4 0.4 copy.14
  162.8 0.6 gather_fusion.1
  163.4 0.0 copy-start.2
  163.4 10.2 %fusion.23 = f32[12,1024]{1,0:T(8,128)S(1)} fusion(bf16[1,1,8,1024,1024]{4,3,2,1,0:T(8,128)(2,1)} %param.18, bf16[8,12,1024]{2,1,0:T(8,128)(2,1)S(1)} %gather_fusion.1, pred[8]{0:T(512)(128)(4,1)S(1)} %get-tuple-element.6), kind=kOutput, calls=%fused_computation.17 | convolution fusion | flops 201424896 | bytes 17022984 | tf_op jit(solution)/shard_map/rnpq,krnq->krp/dot_general | solution.py:60
  173.6 0.0 copy-done.2
  173.7 0.7 fusion.26
  174.3 0.0 copy-done.4
  174.3 0.0 copy-done.6
  174.3 0.1 subtract_reduce_fusion
  174.5 0.0 copy-start.5
  174.5 6.7 %scatter_custom_fusion = f32[1280]{0:T(1024)S(1)} fusion(s32[1024]{0:T(1024)} %bitcast.96, f32[1024]{0:T(1024)S(1)} %broadcast_multiply_fusion, f32[]{:T(128)} %constant.112.clone.1), kind=kCustom, calls=%fused_computation.44 | custom fusion | flops 1024 | bytes 5632 | tf_op jit(solution)/shard_map/scatter-add | solution.py:68
  181.2 39.2 %all-reduce = f32[1280]{0:T(1024)S(1)} all-reduce(f32[1280]{0:T(1024)S(1)} %scatter_custom_fusion), channel_id=3, replica_groups=mesh['gx'=4,'gy'=8] {'gx','gy'}, use_global_device_ids=true, to_apply=%region_2.4.clone | all-reduce | flops 1280 | bytes 10240
  220.4 0.6 broadcast_multiply_fusion.1
  221.0 0.8 dynamic_slice.3
  221.7 0.8 scatter_custom_fusion.1
  222.6 41.0 %all-reduce.1 = f32[160]{0:T(256)S(1)} all-reduce(f32[160]{0:T(256)S(1)} %scatter_custom_fusion.1), channel_id=4, replica_groups=mesh['gx'=4,'gy'=8] {'gx','gy'}, use_global_device_ids=true, to_apply=%region_4.6.clone | all-reduce | flops 160 | bytes 1280
  263.6 0.6 dynamic-slice_multiply_fusion
  264.1 0.0 copy-done.5
  (9 shorter events, 0.1 us)
Async XLA Ops:
  0.6 89.4 %copy-start = (bf16[1,1,1024,1024]{3,2,1,0:T(8,128)(2,1)S(1)}, bf16[1,1,1024,1024]{3,2,1,0:T(8,128)(2,1)}, u32[]{:S(2)}) copy-start(bf16[1,1,1024,1024]{3,2,1,0:T(8,128)(2,1)} %param.17) | copy-start | bytes 6291460
  0.6 89.4 %copy-start.3 = (f32[3,1,1,1024]{3,2,1,0:T(1,128)S(1)}, f32[3,1,1,1024]{3,2,1,0:T(1,128)}, u32[]{:S(2)}) copy-start(f32[3,1,1,1024]{3,2,1,0:T(1,128)} %param.13) | copy-start | bytes 36868
  89.9 84.4 %copy-start.4 = (f32[1,1,1024]{2,1,0:T(1,128)S(1)}, f32[1,1,1024]{2,1,0:T(1,128)}, u32[]{:S(2)}) copy-start(f32[1,1,1024]{2,1,0:T(1,128)} %param.16) | copy-start | bytes 12292
  89.9 84.4 %copy-start.6 = (f32[4]{0:T(128)S(1)}, f32[4]{0:T(128)}, u32[]{:S(2)}) copy-start(f32[4]{0:T(128)} %param.15) | copy-start | bytes 52
  90.1 72.3 %copy-start.1 = (f32[12,1024]{1,0:T(8,128)}, f32[12,1024]{1,0:T(8,128)S(1)}, u32[]{:S(2)}) copy-start(f32[12,1024]{1,0:T(8,128)S(1)} %broadcast_in_dim.31) | copy-start | bytes 147460
  163.4 10.2 %copy-start.2 = (f32[12,1024]{1,0:T(8,128)S(1)}, f32[12,1024]{1,0:T(8,128)}, u32[]{:S(2)}) copy-start(f32[12,1024]{1,0:T(8,128)} %copy-done.1) | copy-start | bytes 147460
  174.5 89.7 %copy-start.5 = (f32[1024]{0:T(1024)}, f32[1024]{0:T(1024)S(1)}, u32[]{:S(2)}) copy-start(f32[1024]{0:T(1024)S(1)} %broadcast_multiply_fusion) | copy-start | bytes 12292
where the time goes:
time: 265 us; the launch traced here: 264 us
  blocking collectives  227 us (86%)
  matrix products  21.7 us (8%)
  other arithmetic  9.56 us (4%)
  local copies, waits for them, and re-layouts  4.77 us (2%)
    all_gather x2, blocking collectives, fetch_neighbours(): whole = lax.all_gather(sent, ('gx', 'gy'), axis=1, tiled=True)  147 us
    unnamed x2, blocking collectives  80.2 us
    dot_general x2, matrix products, shards(): jnp.einsum('rnpq,krnq->krp', far_views, neighbours, preferred_element_typ...  20.4 us
    scatter-add x1, other arithmetic, shards(): jax.ops.segment_sum(assimilation.reshape(-1), organ_of_patch.reshape(-1),...  6.69 us

commit v1 on v0

v1 whole, which is shorter than its diff:
```python
import functools

import jax
import jax.numpy as jnp
from jax import lax
from jax.experimental import pallas as pl
from jax.experimental.pallas import tpu as pltpu
from jax.sharding import PartitionSpec as P

REACH = 2
SIDE = 2 * REACH + 1
SLOTS = SIDE * SIDE
HALVES = 2
PLANT_LANE = 64
MESH = pl.DeviceIdType.MESH
NT = (((1,), (1,)), ((), ()))


def nt_dot(left, right):
    return lax.dot_general(left, right, NT, preferred_element_type=jnp.float32)


def column(values, rows, width):
    index = lax.broadcasted_iota(jnp.int32, (rows, width), 0)
    out = jnp.full((rows, width), values[0], jnp.float32)
    for i in range(1, rows):
        out = jnp.where(index == i, values[i], out)
    return out


def kernel(
    rows, cols, organs, plants,
    direct, omega, band_sun, air_temp, vcmax, self_view, near_view, near_ids, organ_ref, table_ref,
    assim_ref, share_ref,
    views, own, tiles, msg1, recv1, msg2a, msg2b, recv2a, recv2b,
    table, plant_row, dest_org, dest_pl, lane_org, lane_pl, part, gathered,
    load_sem, send1, got1, send2a, got2a, send2b, got2b, send3, got3,
):
    suns = direct.shape[0]
    bands = omega.shape[0]
    near = near_view.shape[2]
    width = vcmax.shape[-1]
    half = width // HALVES
    quarter = half // 4
    ndev = rows * cols
    row = lax.axis_index("gx")
    col = lax.axis_index("gy")
    me = row * cols + col

    loads = []
    for h in range(HALVES):
        span = pl.ds(h * half, half)
        for n in range(near + 1):
            source = self_view.at[0, 0, span] if n == 0 else near_view.at[0, 0, n - 1, span]
            loads.append(pltpu.make_async_copy(source, views.at[n, span], load_sem.at[h, n]))
    for load in loads:
        load.start()

    barrier = pltpu.get_barrier_semaphore()

    def greet(k, carry):
        peer = lax.rem(me + k, ndev)
        pl.semaphore_signal(barrier, inc=1, device_id=(peer // cols, lax.rem(peer, cols)), device_id_type=MESH)
        return carry

    lax.fori_loop(1, ndev, greet, 0)

    row_lo, row_hi = jnp.maximum(row - REACH, 0), jnp.minimum(row + REACH, rows - 1)
    col_lo, col_hi = jnp.maximum(col - REACH, 0), jnp.minimum(col + REACH, cols - 1)

    def each_neighbour(body):
        def by_row(r, carry):
            def by_col(c, inner):
                @pl.when((r != row) | (c != col))
                def _():
                    body(r, c)
                return inner
            return lax.fori_loop(col_lo, col_hi + 1, by_col, carry)
        lax.fori_loop(row_lo, row_hi + 1, by_row, 0)

    def exchange(message, slots, send_sem, got_sem, r, c, outgoing):
        there = (row - r + REACH) * SIDE + (col - c + REACH)
        here = (r - row + REACH) * SIDE + (c - col + REACH)
        return pltpu.make_async_remote_copy(
            src_ref=message, dst_ref=slots.at[there if outgoing else here],
            send_sem=send_sem.at[there], recv_sem=got_sem.at[there if outgoing else here],
            device_id=(r, c), device_id_type=MESH,
        )

    def send(*buffers):
        each_neighbour(lambda r, c: exchange(*buffers, r, c, True).start())

    def receive(*buffers):
        each_neighbour(lambda r, c: exchange(*buffers, r, c, False).wait_recv())

    def sent(*buffers):
        each_neighbour(lambda r, c: exchange(*buffers, r, c, True).wait_send())

    first = (msg1, recv1, send1, got1)
    second = ((msg2a, recv2a, send2a, got2a), (msg2b, recv2b, send2b, got2b))

    own[...] = jnp.zeros_like(own)
    for s in range(suns):
        own[s:s + 1, :] = direct[s, 0]
    for b in range(bands):
        own[suns + b:suns + b + 1, :] = omega[b, 0]
    own_tile = own[...]
    msg1[...] = jnp.concatenate([own_tile[:, :half], own_tile[:, half:]], axis=0).astype(jnp.bfloat16)
    tiles[0] = own_tile

    pl.semaphore_wait(barrier, ndev - 1)
    send(*first)

    table[...] = jnp.zeros_like(table)
    table[0:table_ref.shape[0], :] = table_ref[...]
    entries = table[...]
    level = lax.broadcasted_iota(jnp.int32, entries.shape, 0)
    for j in range(width // 128):
        ids = organ_ref[0, :, j * 128:(j + 1) * 128]
        low = jnp.broadcast_to(ids & 127, entries.shape)
        picked = jnp.take_along_axis(entries, low, axis=1)
        picked = jnp.where(level == (ids >> 7), picked, 0).astype(jnp.float32)
        plant_row[:, j * 128:(j + 1) * 128] = jnp.sum(picked, axis=0, keepdims=True)
    for ids, total, base, dest_ref, lane_ref in (
        (organ_ref[0].astype(jnp.float32), organs, 0, dest_org, lane_org),
        (plant_row[...], plants, PLANT_LANE, dest_pl, lane_pl),
    ):
        share = total // ndev
        dest = jnp.floor((ids + 0.5) * (1.0 / share))
        lane = ids - dest * share + base
        at_row = lax.broadcasted_iota(jnp.int32, (ndev, width), 0).astype(jnp.float32)
        dest_ref[...] = jnp.where(at_row == dest, 1.0, 0.0)
        at_lane = lax.broadcasted_iota(jnp.int32, (128, width), 0).astype(jnp.float32)
        lane_ref[...] = jnp.where(at_lane == lane, 1.0, 0.0).astype(jnp.bfloat16)

    slot_of = []
    for n in range(near):
        block = near_ids[0, 0, n]
        place = (block // cols - row + REACH) * SIDE + (lax.rem(block, cols) - col + REACH)
        slot_of.append(jnp.clip(place, 0, SLOTS - 1))

    own_low = own_tile.astype(jnp.bfloat16)
    once = []
    for h in range(HALVES):
        span = slice(h * half, (h + 1) * half)
        loads[h * (near + 1)].wait()
        total = nt_dot(own_low, views[0, span, :])
        if h == 0:
            receive(*first)
            for n in range(near):
                arrived = recv1[slot_of[n]].astype(jnp.float32)
                tiles[n + 1] = jnp.concatenate([arrived[0:8], arrived[8:16]], axis=1)
        for n in range(1, near + 1):
            loads[h * (near + 1) + n].wait()
            total = total + nt_dot(tiles[n].astype(jnp.bfloat16), views[n, span, :])
        total = total[0:suns]
        once.append(total)
        packed = jnp.concatenate([total[:, i * quarter:(i + 1) * quarter] for i in range(4)], axis=0)
        second[h][0][...] = packed.astype(jnp.bfloat16)
        send(*second[h])

    def second_input(n, h, light):
        span = slice(h * half, (h + 1) * half)
        scaled = [tiles[n, suns + b:suns + b + 1, span] * light for b in range(bands)]
        scaled.append(jnp.zeros((16 - suns * bands, half), jnp.float32))
        return jnp.concatenate(scaled, axis=0).astype(jnp.bfloat16)

    twice = None
    for h in range(HALVES):
        term = nt_dot(second_input(0, h, once[h]), views[0, :, h * half:(h + 1) * half])
        twice = term if twice is None else twice + term
    for h in range(HALVES):
        receive(*second[h])
        for n in range(1, near + 1):
            arrived = second[h][1][slot_of[n - 1]].astype(jnp.float32)
            light = jnp.concatenate([arrived[4 * i:4 * i + 4] for i in range(4)], axis=1)
            twice = twice + nt_dot(second_input(n, h, light), views[n, :, h * half:(h + 1) * half])

    base = own[0:suns, :] + jnp.concatenate(once, axis=1)
    absorbed = []
    for b in range(bands):
        factor = column([band_sun[b, s] for s in range(suns)], suns, width)
        gathered_light = factor * (base + twice[b * suns:(b + 1) * suns])
        absorbed.append((1.0 - own[suns + b:suns + b + 1, :]) * gathered_light)
    air = column([air_temp[s] for s in range(suns)], suns, width)
    leaf_temp = air + 6.0 * (absorbed[1] + absorbed[2])
    capacity = vcmax[0] * jnp.exp(0.07 * (leaf_temp - 25.0))
    jmax = 1.7 * capacity
    light = 1.5 * absorbed[0]
    total = light + jmax
    elec = (total - jnp.sqrt(total * total - 2.8 * light * jmax)) * (1.0 / 1.4)
    carbox = capacity * ((0.7 - 0.05) / (0.7 + 0.5))
    electron = elec * ((0.7 - 0.05) / (0.7 + 0.1))
    net_rate = jnp.minimum(carbox, electron) - 0.015 * capacity
    assim = 0.25 * jnp.sum(net_rate, axis=0, keepdims=True)
    assim_ref[0] = assim

    high = assim.astype(jnp.bfloat16).astype(jnp.float32)
    rest = assim - high
    middle = rest.astype(jnp.bfloat16).astype(jnp.float32)
    low = rest - middle
    sums = None
    for dest_ref, lane_ref in ((dest_org, lane_org), (dest_pl, lane_pl)):
        dest = dest_ref[...]
        stacked = jnp.concatenate([dest * high, dest * middle, dest * low], axis=0).astype(jnp.bfloat16)
        found = nt_dot(stacked, lane_ref[...])
        sums = found if sums is None else sums + found
    sums = sums[0:ndev] + sums[ndev:2 * ndev] + sums[2 * ndev:3 * ndev]
    part[...] = sums

    def hand(k, outgoing):
        peer = lax.rem(me + k, ndev)
        origin = me if outgoing else peer
        return pltpu.make_async_remote_copy(
            src_ref=part.at[pl.ds(peer, 1)], dst_ref=gathered.at[pl.ds(origin, 1)],
            send_sem=send3.at[peer], recv_sem=got3.at[origin],
            device_id=(peer // cols, lax.rem(peer, cols)), device_id_type=MESH,
        )

    def over_peers(act):
        def step(k, carry):
            act(k)
            return carry
        lax.fori_loop(1, ndev, step, 0)

    over_peers(lambda k: hand(k, True).start())
    gathered[pl.ds(me, 1), :] = part[pl.ds(me, 1), :]
    sent(*first)
    sent(*second[0])
    sent(*second[1])
    over_peers(lambda k: hand(k, False).wait_recv())
    share_ref[...] = jnp.sum(gathered[...], axis=0, keepdims=True)
    over_peers(lambda k: hand(k, True).wait_send())


def shards(
    direct, omega, band_sun, air_temp, vcmax, self_view, near_view, near_ids, organ_of_patch, organ_plant,
    *, rows, cols, plants,
):
    ndev = rows * cols
    organs = organ_plant.shape[0]
    near = near_ids.shape[-1]
    width = vcmax.shape[-1]
    levels = organs // 128
    padded = (levels + 7) // 8 * 8
    vmem = pl.BlockSpec(memory_space=pltpu.VMEM)
    smem = pl.BlockSpec(memory_space=pltpu.SMEM)
    hbm = pl.BlockSpec(memory_space=pl.ANY)
    f32, bf16 = jnp.float32, jnp.bfloat16
    slot_sems = pltpu.SemaphoreType.DMA((SLOTS,))
    peer_sems = pltpu.SemaphoreType.DMA((ndev,))
    assimilation, share = pl.pallas_call(
        functools.partial(kernel, rows, cols, organs, plants),
        out_shape=(
            jax.ShapeDtypeStruct((1, 1, width), f32),
            jax.ShapeDtypeStruct((1, 128), f32),
        ),
        in_specs=[vmem, vmem, smem, smem, vmem, hbm, hbm, smem, vmem, vmem],
        out_specs=(vmem, vmem),
        scratch_shapes=[
            pltpu.VMEM((near + 1, width, width), bf16),
            pltpu.VMEM((8, width), f32),
            pltpu.VMEM((near + 1, 8, width), f32),
            pltpu.VMEM((16, width // 2), bf16),
            pltpu.VMEM((SLOTS, 16, width // 2), bf16),
            pltpu.VMEM((16, width // 8), bf16),
            pltpu.VMEM((16, width // 8), bf16),
            pltpu.VMEM((SLOTS, 16, width // 8), bf16),
            pltpu.VMEM((SLOTS, 16, width // 8), bf16),
            pltpu.VMEM((padded, 128), jnp.int32),
            pltpu.VMEM((1, width), f32),
            pltpu.VMEM((ndev, width), f32),
            pltpu.VMEM((ndev, width), f32),
            pltpu.VMEM((128, width), bf16),
            pltpu.VMEM((128, width), bf16),
            pltpu.VMEM((ndev, 128), f32),
            pltpu.VMEM((ndev, 128), f32),
            pltpu.SemaphoreType.DMA((HALVES, near + 1)),
            slot_sems, slot_sems, slot_sems, slot_sems, slot_sems, slot_sems,
            peer_sems, peer_sems,
        ],
        compiler_params=pltpu.CompilerParams(
            collective_id=0, has_side_effects=True, vmem_limit_bytes=56 * 2**20
        ),
        name="canopy",
    )(
        direct, omega, band_sun, air_temp, vcmax, self_view, near_view, near_ids, organ_of_patch,
        organ_plant.reshape(levels, 128),
    )
    organ_share, plant_share = organs // ndev, plants // ndev
    organ_carbon = 0.25 * share[0, :organ_share]
    plant_carbon = share[0, PLANT_LANE:PLANT_LANE + plant_share] / 32.0
    return assimilation, organ_carbon, plant_carbon


def solution(mesh):
    rows, cols = mesh.shape["gx"], mesh.shape["gy"]

    def whole(*args):
        plants = args[9].shape[0] // 8
        return jax.shard_map(
            functools.partial(shards, rows=rows, cols=cols, plants=plants),
            mesh=mesh,
            in_specs=(
                P(None, "gx", "gy", None),
                P(None, "gx", "gy", None),
                P(),
                P(),
                P("gx", "gy", None),
                P("gx", "gy", None, None),
                P("gx", "gy", None, None, None),
                P("gx", "gy", None),
                P("gx", "gy", None),
                P(),
            ),
            out_specs=(P("gx", "gy", None), P(("gx", "gy")), P(("gx", "gy"))),
            check_vma=False,
        )(*args)

    return whole
```

time: 265 us -> 36.1 us (0.14)
  blocking collectives: 227 us -> 0 us
  Pallas kernels: 0 us -> 31.5 us
  matrix products: 21.7 us -> 0 us
  other arithmetic: 9.56 us -> 2.35 us
  local copies, waits for them, and re-layouts: 4.77 us -> 1.26 us
    all_gather x2 -> x0, blocking collectives: 147 us -> none  [fetch_neighbours(): whole = lax.all_gather(sent, ('gx', 'gy'), axis=1, tiled=True)]
    unnamed x2 -> x0, blocking collectives: 80.2 us -> none
    pallas_call x0 -> x1, Pallas kernels: none -> 31.5 us  [shards(): pl.pallas_call(functools.partial(kernel, rows, cols, organs, plants), out...]
    dot_general x4 -> x0, matrix products: 21.7 us -> none  [the longest x2 20.4 us: shards(): jnp.einsum('rnpq,krnq->krp', far_views, neighbours, preferred_element_typ...]
    scatter-add x2 -> x0, other arithmetic: 7.52 us -> none  [the longest x1 6.69 us: shards(): jax.ops.segment_sum(assimilation.reshape(-1), organ_of_patch.reshape(-1),...]
where the time goes in v1:
time: 36.1 us; the launch traced here: 35.8 us
  Pallas kernels  31.5 us (87%)
  other arithmetic  2.35 us (7%)
  local copies, waits for them, and re-layouts  1.26 us (3%)
  between operations  0.64 us (2%)
    pallas_call x1, Pallas kernels, shards(): pl.pallas_call(functools.partial(kernel, rows, cols, organs, plants), out...  31.5 us
    unnamed x1, local copies, waits for them, and re-layouts  1.26 us
    div x1, other arithmetic, shards(): plant_carbon = share[0, PLANT_LANE:PLANT_LANE + plant_share] / 32.0  1.21 us
    mul x1, other arithmetic, shards(): organ_carbon = 0.25 * share[0, :organ_share]  1.14 us

profile of v1, /device:TPU:0, one launch (start us, length us, event | category | flops | bytes accessed | tf_op | source)
XLA Modules:
  0.0 35.8 jit_solution(12623038537738769842)
XLA Ops:
  0.6 31.5 %canopy.1 = (f32[1,1,1024]{2,1,0:T(1,128)}, f32[1,128]{1,0:T(1,128)}) custom-call(f32[4,1,1,1024]{3,2,1,0:T(1,128)} %direct.1, f32[3,1,1,1024]{3,2,1,0:T(1,128)} %omega.1, f32[3,4]{1,0:T(4,128)} %band_sun.1, f32[4]{0:T(128)} %air_temp.1, f32[1,1,1024]{2,1,0:T(1,128)} %vcmax.1, bf16[1,1,1024,1024]{3,2,1,0:T(8,128)(2,1)} %self_view.1, ...), custom_call_target="tpu_custom_call" | custom-call | tf_op jit(solution)/shard_map/canopy/pallas_call | solution.py:252
  32.2 1.2 %multiply_bitcast_fusion = f32[5]{0:T(128)} fusion(f32[1,128]{1,0:T(1,128)} %get-tuple-element.6), kind=kLoop, calls=%fused_computation | loop fusion | flops 5 | bytes 40 | tf_op jit(solution)/shard_map/div | solution.py:292
  33.4 1.1 %multiply_bitcast_fusion.1 = f32[40]{0:T(128)} fusion(f32[1,128]{1,0:T(1,128)} %get-tuple-element.6), kind=kLoop, calls=%fused_computation.1 | loop fusion | flops 40 | bytes 320 | tf_op jit(solution)/shard_map/mul | solution.py:291
  34.5 1.3 %copy.14 = f32[1,1,1024]{2,1,0:T(1,128)} copy(f32[1,1,1024]{2,1,0:T(1,128)} %get-tuple-element.10) | data formatting | bytes 8192

commit v2 on v1

--- a/solution.py
+++ b/solution.py
@@ -30,16 +30,18 @@
 
 def kernel(
     rows, cols, organs, plants,
-    direct, omega, band_sun, air_temp, vcmax, self_view, near_view, near_ids, organ_ref, table_ref,
+    direct, omega, band_sun_in, air_temp_in, vcmax_in, self_view, near_view, near_ids_in, organ_in, table_in,
     assim_ref, share_ref,
-    views, own, tiles, msg1, recv1, msg2a, msg2b, recv2a, recv2b,
+    views, own, tiles, msg1, msg0, recv1, recv0, msg2a, msg2b, recv2a, recv2b,
     table, plant_row, dest_org, dest_pl, lane_org, lane_pl, part, gathered,
-    load_sem, send1, got1, send2a, got2a, send2b, got2b, send3, got3,
+    band_sun, air_temp, vcmax, near_ids, organ_ref,
+    load_sem, small_sem, send1, got1, send0, got0, send2a, got2a, send2b, got2b, send3, got3,
 ):
     suns = direct.shape[0]
     bands = omega.shape[0]
     near = near_view.shape[2]
     width = vcmax.shape[-1]
+    levels = table_in.shape[0]
     half = width // HALVES
     quarter = half // 4
     ndev = rows * cols
@@ -47,23 +49,37 @@
     col = lax.axis_index("gy")
     me = row * cols + col
 
-    loads = []
-    for h in range(HALVES):
+    own[suns + bands:, :] = jnp.zeros((own.shape[0] - suns - bands, width), jnp.float32)
+    table[...] = jnp.zeros_like(table)
+    pairs = [(direct.at[s, 0], own.at[pl.ds(s, 1)]) for s in range(suns)]
+    pairs += [(omega.at[b, 0], own.at[pl.ds(suns + b, 1)]) for b in range(bands)]
+    pairs += [
+        (near_ids_in, near_ids), (organ_in, organ_ref), (table_in, table.at[pl.ds(0, levels)]),
+        (vcmax_in, vcmax), (band_sun_in, band_sun), (air_temp_in, air_temp),
+    ]
+    smalls = [pltpu.make_async_copy(a, b, small_sem.at[i]) for i, (a, b) in enumerate(pairs)]
+    for small in smalls:
+        small.start()
+    loads = {}
+    for h, n in [(h, 0) for h in range(HALVES)] + [(h, n) for h in range(HALVES) for n in range(1, near + 1)]:
         span = pl.ds(h * half, half)
-        for n in range(near + 1):
-            source = self_view.at[0, 0, span] if n == 0 else near_view.at[0, 0, n - 1, span]
-            loads.append(pltpu.make_async_copy(source, views.at[n, span], load_sem.at[h, n]))
-    for load in loads:
-        load.start()
+        source = self_view.at[0, 0, span] if n == 0 else near_view.at[0, 0, n - 1, span]
+        loads[h, n] = pltpu.make_async_copy(source, views.at[n, span], load_sem.at[h, n])
+        loads[h, n].start()
 
     barrier = pltpu.get_barrier_semaphore()
 
-    def greet(k, carry):
-        peer = lax.rem(me + k, ndev)
-        pl.semaphore_signal(barrier, inc=1, device_id=(peer // cols, lax.rem(peer, cols)), device_id_type=MESH)
-        return carry
-
-    lax.fori_loop(1, ndev, greet, 0)
+    def over_peers(act):
+        for i in range(rows):
+            r = lax.rem(row + i, rows)
+
+            def step(j, carry, r=r):
+                act(r, lax.rem(col + j, cols))
+                return carry
+
+            lax.fori_loop(1 if i == 0 else 0, cols, step, 0)
+
+    over_peers(lambda r, c: pl.semaphore_signal(barrier, inc=1, device_id=(r, c), device_id_type=MESH))
 
     row_lo, row_hi = jnp.maximum(row - REACH, 0), jnp.minimum(row + REACH, rows - 1)
     col_lo, col_hi = jnp.maximum(col - REACH, 0), jnp.minimum(col + REACH, cols - 1)
@@ -97,22 +113,29 @@
         each_neighbour(lambda r, c: exchange(*buffers, r, c, True).wait_send())
 
     first = (msg1, recv1, send1, got1)
+    albedos = (msg0, recv0, send0, got0)
     second = ((msg2a, recv2a, send2a, got2a), (msg2b, recv2b, send2b, got2b))
 
-    own[...] = jnp.zeros_like(own)
-    for s in range(suns):
-        own[s:s + 1, :] = direct[s, 0]
-    for b in range(bands):
-        own[suns + b:suns + b + 1, :] = omega[b, 0]
+    def packed(values):
+        step = values.shape[1] // 4
+        return jnp.concatenate([values[:, i * step:(i + 1) * step] for i in range(4)], axis=0).astype(jnp.bfloat16)
+
+    def unpacked(message):
+        values = message.astype(jnp.float32)
+        return jnp.concatenate([values[4 * i:4 * i + 4] for i in range(4)], axis=1)
+
+    for small in smalls[:suns + bands]:
+        small.wait()
     own_tile = own[...]
-    msg1[...] = jnp.concatenate([own_tile[:, :half], own_tile[:, half:]], axis=0).astype(jnp.bfloat16)
-    tiles[0] = own_tile
+    msg1[...] = packed(own_tile[0:4])
+    msg0[...] = packed(own_tile[4:8])
 
     pl.semaphore_wait(barrier, ndev - 1)
     send(*first)
-
-    table[...] = jnp.zeros_like(table)
-    table[0:table_ref.shape[0], :] = table_ref[...]
+    send(*albedos)
+    for small in smalls[suns + bands:]:
+        small.wait()
+
     entries = table[...]
     level = lax.broadcasted_iota(jnp.int32, entries.shape, 0)
     for j in range(width // 128):
@@ -136,45 +159,46 @@
     slot_of = []
     for n in range(near):
         block = near_ids[0, 0, n]
-        place = (block // cols - row + REACH) * SIDE + (lax.rem(block, cols) - col + REACH)
+        place = (lax.div(block, cols) - row + REACH) * SIDE + (lax.rem(block, cols) - col + REACH)
         slot_of.append(jnp.clip(place, 0, SLOTS - 1))
 
-    own_low = own_tile.astype(jnp.bfloat16)
+    own_low = own_tile[0:suns].astype(jnp.bfloat16)
+    totals = []
+    for h in range(HALVES):
+        loads[h, 0].wait()
+        totals.append(nt_dot(own_low, views[0, h * half:(h + 1) * half, :]))
+    receive(*first)
+    for n in range(near):
+        tiles[n, 0:4, :] = unpacked(recv1[slot_of[n]])
     once = []
     for h in range(HALVES):
         span = slice(h * half, (h + 1) * half)
-        loads[h * (near + 1)].wait()
-        total = nt_dot(own_low, views[0, span, :])
-        if h == 0:
-            receive(*first)
-            for n in range(near):
-                arrived = recv1[slot_of[n]].astype(jnp.float32)
-                tiles[n + 1] = jnp.concatenate([arrived[0:8], arrived[8:16]], axis=1)
+        total = totals[h]
         for n in range(1, near + 1):
-            loads[h * (near + 1) + n].wait()
-            total = total + nt_dot(tiles[n].astype(jnp.bfloat16), views[n, span, :])
-        total = total[0:suns]
+            loads[h, n].wait()
+            total = total + nt_dot(tiles[n - 1, 0:4, :].astype(jnp.bfloat16), views[n, span, :])
         once.append(total)
-        packed = jnp.concatenate([total[:, i * quarter:(i + 1) * quarter] for i in range(4)], axis=0)
-        second[h][0][...] = packed.astype(jnp.bfloat16)
+        second[h][0][...] = packed(total)
         send(*second[h])
 
-    def second_input(n, h, light):
+    def second_input(tile, h, light):
         span = slice(h * half, (h + 1) * half)
-        scaled = [tiles[n, suns + b:suns + b + 1, span] * light for b in range(bands)]
+        scaled = [tile[suns + b:suns + b + 1, span] * light for b in range(bands)]
         scaled.append(jnp.zeros((16 - suns * bands, half), jnp.float32))
         return jnp.concatenate(scaled, axis=0).astype(jnp.bfloat16)
 
     twice = None
     for h in range(HALVES):
-        term = nt_dot(second_input(0, h, once[h]), views[0, :, h * half:(h + 1) * half])
+        term = nt_dot(second_input(own, h, once[h]), views[0, :, h * half:(h + 1) * half])
         twice = term if twice is None else twice + term
+    receive(*albedos)
+    for n in range(near):
+        tiles[n, 4:8, :] = unpacked(recv0[slot_of[n]])
     for h in range(HALVES):
         receive(*second[h])
         for n in range(1, near + 1):
-            arrived = second[h][1][slot_of[n - 1]].astype(jnp.float32)
-            light = jnp.concatenate([arrived[4 * i:4 * i + 4] for i in range(4)], axis=1)
-            twice = twice + nt_dot(second_input(n, h, light), views[n, :, h * half:(h + 1) * half])
+            light = unpacked(second[h][1][slot_of[n - 1]])
+            twice = twice + nt_dot(second_input(tiles.at[n - 1], h, light), views[n, :, h * half:(h + 1) * half])
 
     base = own[0:suns, :] + jnp.concatenate(once, axis=1)
     absorbed = []
@@ -208,29 +232,29 @@
     sums = sums[0:ndev] + sums[ndev:2 * ndev] + sums[2 * ndev:3 * ndev]
     part[...] = sums
 
-    def hand(k, outgoing):
-        peer = lax.rem(me + k, ndev)
-        origin = me if outgoing else peer
-        return pltpu.make_async_remote_copy(
-            src_ref=part.at[pl.ds(peer, 1)], dst_ref=gathered.at[pl.ds(origin, 1)],
-            send_sem=send3.at[peer], recv_sem=got3.at[origin],
-            device_id=(peer // cols, lax.rem(peer, cols)), device_id_type=MESH,
-        )
-
-    def over_peers(act):
-        def step(k, carry):
-            act(k)
-            return carry
-        lax.fori_loop(1, ndev, step, 0)
-
-    over_peers(lambda k: hand(k, True).start())
-    gathered[pl.ds(me, 1), :] = part[pl.ds(me, 1), :]
+    def hand(r, c):
+        peer = r * cols + c
+        pltpu.make_async_remote_copy(
+            src_ref=part.at[pl.ds(peer, 1)], dst_ref=gathered.at[pl.ds(me, 1)],
+            send_sem=send3, recv_sem=got3, device_id=(r, c), device_id_type=MESH,
+        ).start()
+
+    over_peers(hand)
+    pltpu.make_async_copy(part.at[pl.ds(me, 1)], gathered.at[pl.ds(me, 1)], got3).start()
     sent(*first)
+    sent(*albedos)
     sent(*second[0])
     sent(*second[1])
-    over_peers(lambda k: hand(k, False).wait_recv())
+    pltpu.make_async_copy(part, gathered, got3).wait()
     share_ref[...] = jnp.sum(gathered[...], axis=0, keepdims=True)
-    over_peers(lambda k: hand(k, True).wait_send())
+    others = pl.ds(0, ndev - 1)
+    pltpu.make_async_copy(part.at[others], gathered.at[others], send3).wait()
+
+
+def finish(organ_share, plant_share, assim_in, share_in, assim_ref, organ_ref, plant_ref):
+    assim_ref[...] = assim_in[...]
+    organ_ref[...] = 0.25 * share_in[:, 0:organ_share]
+    plant_ref[...] = share_in[:, PLANT_LANE:PLANT_LANE + plant_share] * (1.0 / 32.0)
 
 
 def shards(
@@ -244,25 +268,25 @@
     levels = organs // 128
     padded = (levels + 7) // 8 * 8
     vmem = pl.BlockSpec(memory_space=pltpu.VMEM)
-    smem = pl.BlockSpec(memory_space=pltpu.SMEM)
     hbm = pl.BlockSpec(memory_space=pl.ANY)
     f32, bf16 = jnp.float32, jnp.bfloat16
     slot_sems = pltpu.SemaphoreType.DMA((SLOTS,))
-    peer_sems = pltpu.SemaphoreType.DMA((ndev,))
     assimilation, share = pl.pallas_call(
         functools.partial(kernel, rows, cols, organs, plants),
         out_shape=(
             jax.ShapeDtypeStruct((1, 1, width), f32),
             jax.ShapeDtypeStruct((1, 128), f32),
         ),
-        in_specs=[vmem, vmem, smem, smem, vmem, hbm, hbm, smem, vmem, vmem],
+        in_specs=[hbm] * 10,
         out_specs=(vmem, vmem),
         scratch_shapes=[
             pltpu.VMEM((near + 1, width, width), bf16),
             pltpu.VMEM((8, width), f32),
-            pltpu.VMEM((near + 1, 8, width), f32),
-            pltpu.VMEM((16, width // 2), bf16),
-            pltpu.VMEM((SLOTS, 16, width // 2), bf16),
+            pltpu.VMEM((near, 8, width), f32),
+            pltpu.VMEM((16, width // 4), bf16),
+            pltpu.VMEM((16, width // 4), bf16),
+            pltpu.VMEM((SLOTS, 16, width // 4), bf16),
+            pltpu.VMEM((SLOTS, 16, width // 4), bf16),
             pltpu.VMEM((16, width // 8), bf16),
             pltpu.VMEM((16, width // 8), bf16),
             pltpu.VMEM((SLOTS, 16, width // 8), bf16),
@@ -275,9 +299,15 @@
             pltpu.VMEM((128, width), bf16),
             pltpu.VMEM((ndev, 128), f32),
             pltpu.VMEM((ndev, 128), f32),
+            pltpu.SMEM(band_sun.shape, f32),
+            pltpu.SMEM(air_temp.shape, f32),
+            pltpu.VMEM(vcmax.shape, f32),
+            pltpu.SMEM(near_ids.shape, jnp.int32),
+            pltpu.VMEM(organ_of_patch.shape, jnp.int32),
             pltpu.SemaphoreType.DMA((HALVES, near + 1)),
-            slot_sems, slot_sems, slot_sems, slot_sems, slot_sems, slot_sems,
-            peer_sems, peer_sems,
+            pltpu.SemaphoreType.DMA((16,)),
+            slot_sems, slot_sems, slot_sems, slot_sems, slot_sems, slot_sems, slot_sems, slot_sems,
+            pltpu.SemaphoreType.DMA, pltpu.SemaphoreType.DMA,
         ],
         compiler_params=pltpu.CompilerParams(
             collective_id=0, has_side_effects=True, vmem_limit_bytes=56 * 2**20
@@ -288,9 +318,19 @@
         organ_plant.reshape(levels, 128),
     )
     organ_share, plant_share = organs // ndev, plants // ndev
-    organ_carbon = 0.25 * share[0, :organ_share]
-    plant_carbon = share[0, PLANT_LANE:PLANT_LANE + plant_share] / 32.0
-    return assimilation, organ_carbon, plant_carbon
+    assimilation, organ_carbon, plant_carbon = pl.pallas_call(
+        functools.partial(finish, organ_share, plant_share),
+        out_shape=(
+            jax.ShapeDtypeStruct((1, 1, width), f32),
+            jax.ShapeDtypeStruct((1, organ_share), f32),
+            jax.ShapeDtypeStruct((1, plant_share), f32),
+        ),
+        in_specs=[vmem, vmem],
+        out_specs=(vmem, vmem, vmem),
+        compiler_params=pltpu.CompilerParams(vmem_limit_bytes=60 * 2**20),
+        name="finish",
+    )(assimilation, share)
+    return assimilation, organ_carbon.reshape(-1), plant_carbon.reshape(-1)
 
 
 def solution(mesh):

time: 36.1 us -> 32.3 us (0.89)
  other arithmetic: 2.35 us -> 0 us
  local copies, waits for them, and re-layouts: 1.26 us -> 0 us
    pallas_call x1, Pallas kernels: 31.5 us -> 30.2 us  [shards(): pl.pallas_call(functools.partial(kernel, rows, cols, organs, plants), out...]
    pallas_call x0 -> x1, Pallas kernels: none -> 1.27 us  [shards(): pl.pallas_call(functools.partial(finish, organ_share, plant_share), out_s...]
    unnamed x1 -> x0, local copies, waits for them, and re-layouts: 1.26 us -> none
    div x1 -> x0, other arithmetic: 1.21 us -> none  [shards(): plant_carbon = share[0, PLANT_LANE:PLANT_LANE + plant_share] / 32.0]
    mul x1 -> x0, other arithmetic: 1.14 us -> none  [shards(): organ_carbon = 0.25 * share[0, :organ_share]]
where the time goes in v2:
time: 32.3 us; the launch traced here: 32.1 us
  Pallas kernels  31.4 us (97%)
  between operations  0.64 us (2%)
    pallas_call x1, Pallas kernels, shards(): pl.pallas_call(functools.partial(kernel, rows, cols, organs, plants), out...  30.2 us
    pallas_call x1, Pallas kernels, shards(): pl.pallas_call(functools.partial(finish, organ_share, plant_share), out_s...  1.27 us

profile of v2, /device:TPU:0, one launch (start us, length us, event | category | flops | bytes accessed | tf_op | source)
XLA Modules:
  0.0 32.1 jit_solution(8607000978445254811)
XLA Ops:
  0.6 30.2 %canopy.1 = (f32[1,1,1024]{2,1,0:T(1,128)}, f32[1,128]{1,0:T(1,128)}) custom-call(f32[4,1,1,1024]{3,2,1,0:T(1,128)} %direct.1, f32[3,1,1,1024]{3,2,1,0:T(1,128)} %omega.1, f32[3,4]{1,0:T(4,128)} %band_sun_in.1, f32[4]{0:T(128)} %air_temp_in.1, f32[1,1,1024]{2,1,0:T(1,128)} %vcmax_in.1, bf16[1,1,1024,1024]{3,2,1,0:T(8,128)(2,1)} %self_view.1, ...), custom_call_target="tpu_custom_call" | custom-call | tf_op jit(solution)/shard_map/canopy/pallas_call | solution.py:274
  30.8 1.3 %finish.1 = (f32[1,1,1024]{2,1,0:T(1,128)}, f32[1,40]{1,0:T(1,128)}, f32[1,5]{1,0:T(1,128)}) custom-call(f32[1,1,1024]{2,1,0:T(1,128)} %get-tuple-element.8.assim_in, f32[1,128]{1,0:T(1,128)} %get-tuple-element.9.share_in), custom_call_target="tpu_custom_call" | custom-call | tf_op jit(solution)/shard_map/finish/pallas_call | solution.py:321

commit v3 on v2

--- a/solution.py
+++ b/solution.py
@@ -176,6 +176,7 @@
         total = totals[h]
         for n in range(1, near + 1):
             loads[h, n].wait()
+        for n in range(1, near + 1):
             total = total + nt_dot(tiles[n - 1, 0:4, :].astype(jnp.bfloat16), views[n, span, :])
         once.append(total)
         second[h][0][...] = packed(total)

time: 32.3 us -> 32.2 us (level)
  no operation moved by 1% of the time
where the time goes in v3:
time: 32.2 us; the launch traced here: 32 us
  Pallas kernels  31.4 us (98%)
  between operations  0.64 us (2%)
    pallas_call x1, Pallas kernels, shards(): pl.pallas_call(functools.partial(kernel, rows, cols, organs, plants), out...  30.1 us
    pallas_call x1, Pallas kernels, shards(): pl.pallas_call(functools.partial(finish, organ_share, plant_share), out_s...  1.27 us

profile of v3, /device:TPU:0, one launch (start us, length us, event | category | flops | bytes accessed | tf_op | source)
XLA Modules:
  0.0 32.0 jit_solution(817354488936342151)
XLA Ops:
  0.6 30.1 %canopy.1 = (f32[1,1,1024]{2,1,0:T(1,128)}, f32[1,128]{1,0:T(1,128)}) custom-call(f32[4,1,1,1024]{3,2,1,0:T(1,128)} %direct.1, f32[3,1,1,1024]{3,2,1,0:T(1,128)} %omega.1, f32[3,4]{1,0:T(4,128)} %band_sun_in.1, f32[4]{0:T(128)} %air_temp_in.1, f32[1,1,1024]{2,1,0:T(1,128)} %vcmax_in.1, bf16[1,1,1024,1024]{3,2,1,0:T(8,128)(2,1)} %self_view.1, ...), custom_call_target="tpu_custom_call" | custom-call | tf_op jit(solution)/shard_map/canopy/pallas_call | solution.py:275
  30.7 1.3 %finish.1 = (f32[1,1,1024]{2,1,0:T(1,128)}, f32[1,40]{1,0:T(1,128)}, f32[1,5]{1,0:T(1,128)}) custom-call(f32[1,1,1024]{2,1,0:T(1,128)} %get-tuple-element.8.assim_in, f32[1,128]{1,0:T(1,128)} %get-tuple-element.9.share_in), custom_call_target="tpu_custom_call" | custom-call | tf_op jit(solution)/shard_map/finish/pallas_call | solution.py:322
